TPU v7x, 256 devices: a whole 4x4x8 slice. The times are simulated.
256 devices in a mesh: dp: 32 (over y, z_hi, x), context: 8 (over z_lo, core).
Axes of the slice: x: 4, y: 4, z: 8 (z_hi: 2, z_lo: 4; z = z_hi * 4 + z_lo), core: 2. Of those that a mesh axis runs over, the one named last changes fastest.
Arguments:
- projected: bfloat16 [3, 16384, 4096], P(None, 'context', 'dp'), may hold values from -6 to 6
- filter_taps: bfloat16 [16384, 4096], P('context', 'dp'), may hold values from -0.046875 to 0.046875
- out_grad: bfloat16 [16384, 4096], P('context', 'dp'), may hold values from -6 to 6
- out_weight: bfloat16 [4096, 4096], P('dp', 'context'), may hold values from -0.09375 to 0.09375
Outputs:
- grad_streams: bfloat16 [3, 16384, 4096], P(None, 'context', 'dp')
- grad_filter: float32 [16384, 4096], P('context', 'dp')
- grad_weight: float32 [4096, 4096], P('dp', 'context')
All inputs are finite; a program needn't handle non-finite values.
Results may differ from a plain program's by a relative error of at most 0.017.
Values may be sent and summed in bfloat16 or wider, within the bound.
A program may use at most 128 MiB of HBM per device.

v0:
```python
import math

import jax
import jax.numpy as jnp
from jax import lax
from jax.sharding import PartitionSpec as P

BLOCK = 1024


def angles(leading, trailing, modulus):
    product = leading[:, None] * trailing[None, :] % modulus
    return 2.0 * math.pi / modulus * product.astype(jnp.float32)


def small_table(count_q, sign):
    steps_q = jnp.arange(count_q, dtype=jnp.int32)
    phases = angles(steps_q, steps_q, count_q)
    cosine = jnp.cos(phases)
    sines = sign * jnp.sin(phases)
    upper = jnp.stack([cosine, sines], 1)
    lower = jnp.stack([-sines, cosine], 1)
    return jnp.stack([upper, lower], 0).astype(jnp.bfloat16)


def spread_forward(signal):
    batches, length_dev, channels = signal.shape
    devices = lax.axis_size("context")
    position = lax.axis_index("context")
    half_block = BLOCK // 2
    per_device_p = half_block // devices
    count_q = length_dev // per_device_p
    local_q = count_q // devices
    total_len = BLOCK * count_q
    blocks = signal.reshape(batches, per_device_p, count_q, channels)
    blocks = lax.all_to_all(blocks, "context", split_axis=2, concat_axis=1, tiled=True)
    phases = angles(
        jnp.arange(BLOCK, dtype=jnp.int32), jnp.arange(half_block, dtype=jnp.int32), BLOCK
    )
    section_table = jnp.concatenate([jnp.cos(phases), -jnp.sin(phases)], 0).astype(jnp.bfloat16)
    partial_sum = jnp.einsum(
        "kp,bpqc->bkqc", section_table, blocks, preferred_element_type=jnp.float32
    )
    real_part = partial_sum[:, :BLOCK]
    imag_part = partial_sum[:, BLOCK:]
    global_q = position * local_q + jnp.arange(local_q, dtype=jnp.int32)
    twist = angles(jnp.arange(BLOCK, dtype=jnp.int32), global_q, total_len)
    cosine = jnp.cos(twist)[:, :, None]
    sines = jnp.sin(twist)[:, :, None]
    turned = jnp.stack(
        [real_part * cosine + imag_part * sines, imag_part * cosine - real_part * sines], 1
    ).astype(jnp.bfloat16)
    turned = lax.all_to_all(turned, "context", split_axis=2, concat_axis=3, tiled=True)
    table_q = small_table(count_q, 1.0)
    spectrum = jnp.einsum("okiq,bipqc->bopkc", table_q, turned, preferred_element_type=jnp.float32)
    return spectrum.astype(jnp.bfloat16)


def spread_inverse(spectrum):
    batches = spectrum.shape[0]
    local_k = spectrum.shape[2]
    count_q = spectrum.shape[3]
    channels = spectrum.shape[4]
    devices = lax.axis_size("context")
    position = lax.axis_index("context")
    half_block = BLOCK // 2
    local_q = count_q // devices
    total_len = BLOCK * count_q
    table_q = small_table(count_q, -1.0)
    partial_sum = jnp.einsum(
        "oqik,bipkc->bopqc", table_q, spectrum, preferred_element_type=jnp.float32
    )
    global_k = position * local_k + jnp.arange(local_k, dtype=jnp.int32)
    twist = angles(global_k, jnp.arange(count_q, dtype=jnp.int32), total_len)
    cosine = jnp.cos(twist)[:, :, None]
    sines = jnp.sin(twist)[:, :, None]
    real_part = partial_sum[:, 0]
    imag_part = partial_sum[:, 1]
    turned = jnp.stack(
        [real_part * cosine - imag_part * sines, imag_part * cosine + real_part * sines], 1
    ).astype(jnp.bfloat16)
    turned = lax.all_to_all(turned, "context", split_axis=3, concat_axis=2, tiled=True)
    phases = angles(
        jnp.arange(half_block, dtype=jnp.int32), jnp.arange(BLOCK, dtype=jnp.int32), BLOCK
    )
    section_table = jnp.concatenate([jnp.cos(phases), -jnp.sin(phases)], 1).astype(jnp.bfloat16)
    merged = turned.reshape(batches, 2 * BLOCK, local_q, channels)
    values = jnp.einsum("pk,bkqc->bpqc", section_table, merged, preferred_element_type=jnp.float32)
    values = (values * (1.0 / total_len)).astype(jnp.bfloat16)
    values = lax.all_to_all(values, "context", split_axis=1, concat_axis=2, tiled=True)
    return values.reshape(batches, values.shape[1] * count_q, channels)


def forward_spectrum(signal):
    result = spread_forward(signal)
    return result


def inverse_spectrum(spectrum):
    result = spread_inverse(spectrum)
    return result


def complex_product(first_spec, second_spec, conjugate):
    first_real = first_spec[:, 0].astype(jnp.float32)
    first_imag = first_spec[:, 1].astype(jnp.float32)
    second_real = second_spec[:, 0].astype(jnp.float32)
    second_imag = second_spec[:, 1].astype(jnp.float32)
    if conjugate:
        real_part = first_real * second_real + first_imag * second_imag
        imag_part = first_real * second_imag - first_imag * second_real
    else:
        real_part = first_real * second_real - first_imag * second_imag
        imag_part = first_real * second_imag + first_imag * second_real
    return jnp.stack([real_part, imag_part], 1).astype(jnp.bfloat16)


def shards(projected, filter_taps, out_grad, out_weight):
    length_dev = projected.shape[1]
    queries = projected[0].astype(jnp.float32)
    key_stream = projected[1].astype(jnp.float32)
    value_stream = projected[2].astype(jnp.float32)
    mixing = (key_stream * value_stream).astype(jnp.bfloat16)
    mixing_spec = forward_spectrum(mixing[None])
    filter_spec = forward_spectrum(filter_taps[None])
    conv = inverse_spectrum(complex_product(filter_spec, mixing_spec, False))[0]
    weight_rows = lax.all_gather(out_weight, "context", axis=1, tiled=True)
    loss_scale = 1.0 / math.sqrt(lax.axis_size("context") * length_dev)
    gathered_cols = lax.all_gather(out_grad, "dp", axis=1, tiled=True)
    upstream = lax.dot_general(
        gathered_cols, weight_rows, (((1,), (1,)), ((), ())), preferred_element_type=jnp.float32
    )
    gated = (upstream * queries).astype(jnp.bfloat16)
    grad_spec = forward_spectrum(gated[None])
    grad_mixing = inverse_spectrum(complex_product(filter_spec, grad_spec, True))[0].astype(
        jnp.float32
    )
    grad_taps = inverse_spectrum(complex_product(mixing_spec, grad_spec, True))[0]
    conv_wide = conv.astype(jnp.float32)
    grads = jnp.stack(
        [upstream * conv_wide, grad_mixing * value_stream, grad_mixing * key_stream]
    ).astype(jnp.bfloat16)
    output = (queries * conv_wide).astype(jnp.bfloat16)
    complete = loss_scale * lax.dot_general(
        output, gathered_cols, (((0,), (0,)), ((), ())), preferred_element_type=jnp.float32
    )
    grad_weight = lax.psum_scatter(
        complete.astype(jnp.bfloat16), "context", scatter_dimension=1, tiled=True
    ).astype(jnp.float32)
    grad_filter = loss_scale * grad_taps.astype(jnp.float32)
    return (grads, grad_filter, grad_weight)


def solution(mesh):
    placed = (P(None, "context", "dp"), P("context", "dp"), P("context", "dp"), P("dp", "context"))
    return jax.shard_map(
        shards,
        mesh=mesh,
        in_specs=placed,
        out_specs=(P(None, "context", "dp"), P("context", "dp"), P("dp", "context")),
        check_vma=False,
    )
```

profile of v0, /device:TPU:41, one launch (start us, length us, event | category | flops | bytes accessed | tf_op | source)
XLA Modules:
  0.0 917.1 jit_solution(9882580969223781703)
XLA Ops:
  10.7 6.3 all-to-all-start
  17.0 29.9 %all-gather.5.cloned.1.call-done = bf16[128,4096]{1,0:T(8,128)(2,1)} async-done(((bf16[128,512]{1,0:T(8,128)(2,1)}), bf16[128,4096]{1,0:T(8,128)(2,1)}) %all-gather.5.cloned.1.call-update) | async-done | bytes 1048592 | tf_op jit(solution)/shard_map/all_gather | solution.py:127
  46.9 354.2 %all-gather.3.cloned.1.call-done = bf16[2048,4096]{1,0:T(8,128)(2,1)} async-done(((bf16[2048,128]{1,0:T(8,128)(2,1)}), bf16[2048,4096]{1,0:T(8,128)(2,1)}) %all-gather.3.cloned.1.call-update) | async-done | bytes 16777232 | tf_op jit(solution)/shard_map/all_gather | solution.py:129
  401.1 11.6 %fusion.41 = (bf16[2048,128]{1,0:T(8,128)(2,1)S(1)}, f32[2048,128]{1,0:T(8,128)}) fusion(bf16[3,2048,128]{2,1,0:T(8,128)(2,1)} %param.4, bf16[2048,4096]{1,0:T(8,128)(2,1)} %all-gather.3.cloned.1.call-done, bf16[128,4096]{1,0:T(8,128)(2,1)} %all-gather.5.cloned.1.call-done), kind=kOutput, calls=%fused_computation.107 | convolution fusion | flops 2148270080 | bytes 19922944 | tf_op jit(solution)/shard_map/dot_general | solution.py:130
  413.7 7.0 all-to-all-start.6
  421.0 8.5 negate_convert_fusion.1
  440.8 7.0 all-to-all-start.1
  452.2 41.1 %all-to-all-done.1 = bf16[1,2,1024,4,128]{4,3,1,0,2:T(4,128)(2,1)S(1)} async-done(((bf16[1,2,1024,4,128]{4,3,1,0,2:T(4,128)(2,1)}), bf16[1,2,1024,4,128]{4,3,1,0,2:T(4,128)(2,1)S(1)}, u32[]{:S(2)}, u32[]{:S(2)}) %all-to-all-start.1) | async-done | bytes 2097184 | tf_op jit(solution)/shard_map/all_to_all | solution.py:53
  493.3 7.8 all-to-all-start.7
  504.3 42.3 %all-to-all-done.7 = bf16[1,2,1024,4,128]{4,3,1,0,2:T(4,128)(2,1)} async-done(((bf16[1,2,1024,4,128]{4,3,1,0,2:T(4,128)(2,1)}), bf16[1,2,1024,4,128]{4,3,1,0,2:T(4,128)(2,1)}, u32[]{:S(2)}, u32[]{:S(2)}) %all-to-all-start.7) | async-done | bytes 2097184 | tf_op jit(solution)/shard_map/all_to_all | solution.py:53
  559.0 8.2 all-to-all-start.8
  567.2 9.2 negate_convert_fusion
  576.4 36.3 %all-to-all-done.8 = bf16[1,2,128,32,128]{4,1,2,0,3:T(2,128)(2,1)} async-done(((bf16[1,2,128,32,128]{4,1,2,0,3:T(2,128)(2,1)}), bf16[1,2,128,32,128]{4,1,2,0,3:T(2,128)(2,1)}, u32[]{:S(2)}, u32[]{:S(2)}) %all-to-all-start.8) | async-done | bytes 2097184 | tf_op jit(solution)/shard_map/all_to_all | solution.py:82
  612.7 4.7 copy.123
  617.4 4.1 reshape.698
  621.5 3.9 fusion.36
  626.8 18.3 %all_to_all.162 = bf16[1,512,4,128]{3,2,0,1:T(4,128)(2,1)S(1)} all-to-all(bf16[1,512,4,128]{3,2,0,1:T(4,128)(2,1)S(1)} %copy.124), channel_id=1, replica_groups=mesh['dp'=32,'context'=8] {'context'}, dimensions={1} | all-to-all | bytes 1048576 | tf_op jit(solution)/shard_map/all_to_all | solution.py:90
  648.1 17.9 %all_to_all.163 = bf16[1,64,32,128]{3,1,0,2:T(8,128)(2,1)S(1)} all-to-all(bf16[1,64,32,128]{3,1,0,2:T(8,128)(2,1)S(1)} %copy.96), channel_id=1, replica_groups=mesh['dp'=32,'context'=8] {'context'}, dimensions={2} | all-to-all | bytes 1048576 | tf_op jit(solution)/shard_map/all_to_all | solution.py:36
  670.5 51.7 %all_to_all.164 = bf16[1,2,1024,4,128]{4,3,1,0,2:T(4,128)(2,1)S(1)} all-to-all(bf16[1,2,1024,4,128]{4,3,1,0,2:T(4,128)(2,1)S(1)} %copy.100), channel_id=1, replica_groups=mesh['dp'=32,'context'=8] {'context'}, dimensions={2} | all-to-all | bytes 4194304 | tf_op jit(solution)/shard_map/all_to_all | solution.py:53
  734.4 6.6 all-to-all-start.4
  745.9 40.6 %all-to-all-done.4 = bf16[1,2,128,32,128]{4,1,2,0,3:T(2,128)(2,1)S(1)} async-done(((bf16[1,2,128,32,128]{4,1,2,0,3:T(2,128)(2,1)}), bf16[1,2,128,32,128]{4,1,2,0,3:T(2,128)(2,1)S(1)}, u32[]{:S(2)}, u32[]{:S(2)}) %all-to-all-start.4) | async-done | bytes 2097184 | tf_op jit(solution)/shard_map/all_to_all | solution.py:82
  787.9 7.1 all-to-all-start.10
  795.0 4.7 copy.107
  799.7 4.2 reshape.695
  803.9 4.0 fusion.37
  810.0 30.4 %all-to-all-done.10 = bf16[1,2,128,32,128]{4,1,2,0,3:T(2,128)(2,1)S(1)} async-done(((bf16[1,2,128,32,128]{4,1,2,0,3:T(2,128)(2,1)}), bf16[1,2,128,32,128]{4,1,2,0,3:T(2,128)(2,1)S(1)}, u32[]{:S(2)}, u32[]{:S(2)}) %all-to-all-start.10) | async-done | bytes 2097184 | tf_op jit(solution)/shard_map/all_to_all | solution.py:82
  840.5 7.6 all-to-all-start.5
  854.3 5.6 all-to-all-done.5
  861.8 9.3 %fusion = bf16[128,4096]{1,0:T(8,128)(2,1)} fusion(bf16[2048,4096]{1,0:T(8,128)(2,1)} %all-gather.3.cloned.1.call-done, f32[2048,128]{1,0:T(8,128)S(1)} %bitcast.271, bf16[3,2048,128]{2,1,0:T(8,128)(2,1)} %param.4), kind=kOutput, calls=%fused_computation.1 | convolution fusion | flops 2149318656 | bytes 19398656 | tf_op jit(solution)/shard_map/dot_general | solution.py:144
  871.1 3.7 fusion.35
  876.2 23.2 %all_to_all.165 = bf16[1,512,4,128]{3,2,0,1:T(4,128)(2,1)S(1)} all-to-all(bf16[1,512,4,128]{3,2,0,1:T(4,128)(2,1)S(1)} %copy.130), channel_id=1, replica_groups=mesh['dp'=32,'context'=8] {'context'}, dimensions={1} | all-to-all | bytes 1048576 | tf_op jit(solution)/shard_map/all_to_all | solution.py:90
  902.6 5.9 reduce-scatter.2.cloned.1.call-done
  (100 shorter events, 79.3 us)
Async XLA Ops:
  7.2 39.8 %all-gather.5.cloned.1.call-start = ((), (), s32[]{:S(2)}) async-start(), calls=%async_computation.14 | async-start | bytes 1179648 | tf_op jit(solution)/shard_map/all_gather | solution.py:127
  7.9 393.2 %all-gather.3.cloned.1.call-start = ((), (), s32[]{:S(2)}) async-start(), calls=%async_computation.13 | async-start | bytes 17301504 | tf_op jit(solution)/shard_map/all_gather | solution.py:129
  10.7 403.0 %all-to-all-start = ((bf16[1,64,32,128]{3,1,0,2:T(8,128)(2,1)}), bf16[1,64,32,128]{3,1,0,2:T(8,128)(2,1)S(1)}, u32[]{:S(2)}, u32[]{:S(2)}) async-start(bf16[1,64,32,128]{3,1,0,2:T(8,128)(2,1)} %copy.91), calls=%async_computation | async-start | bytes 1048576 | tf_op jit(solution)/shard_map/all_to_all | solution.py:36
  413.7 19.1 %all-to-all-start.6 = ((bf16[1,64,32,128]{3,1,0,2:T(8,128)(2,1)}), bf16[1,64,32,128]{3,1,0,2:T(8,128)(2,1)S(1)}, u32[]{:S(2)}, u32[]{:S(2)}) async-start(bf16[1,64,32,128]{3,1,0,2:T(8,128)(2,1)} %copy.111), calls=%async_computation.6 | async-start | bytes 1048576 | tf_op jit(solution)/shard_map/all_to_all | solution.py:36
  429.5 3.3 copy-start.11
  429.5 3.3 copy-start.13
  432.9 2.2 copy-start.4
  440.8 52.5 %all-to-all-start.1 = ((bf16[1,2,1024,4,128]{4,3,1,0,2:T(4,128)(2,1)}), bf16[1,2,1024,4,128]{4,3,1,0,2:T(4,128)(2,1)S(1)}, u32[]{:S(2)}, u32[]{:S(2)}) async-start(bf16[1,2,1024,4,128]{4,3,1,0,2:T(4,128)(2,1)} %copy.93), calls=%async_computation.1 | async-start | bytes 4194304 | tf_op jit(solution)/shard_map/all_to_all | solution.py:53
  493.3 53.3 %all-to-all-start.7 = ((bf16[1,2,1024,4,128]{4,3,1,0,2:T(4,128)(2,1)}), bf16[1,2,1024,4,128]{4,3,1,0,2:T(4,128)(2,1)}, u32[]{:S(2)}, u32[]{:S(2)}) async-start(bf16[1,2,1024,4,128]{4,3,1,0,2:T(4,128)(2,1)} %copy.115), calls=%async_computation.7 | async-start | bytes 4194304 | tf_op jit(solution)/shard_map/all_to_all | solution.py:53
  546.6 2.9 copy-start.3
  551.1 1.3 copy-start
  559.0 53.6 %all-to-all-start.8 = ((bf16[1,2,128,32,128]{4,1,2,0,3:T(2,128)(2,1)}), bf16[1,2,128,32,128]{4,1,2,0,3:T(2,128)(2,1)}, u32[]{:S(2)}, u32[]{:S(2)}) async-start(bf16[1,2,128,32,128]{4,1,2,0,3:T(2,128)(2,1)} %copy.122), calls=%async_computation.8 | async-start | bytes 4194304 | tf_op jit(solution)/shard_map/all_to_all | solution.py:82
  576.4 45.1 %copy-start.9 = (bf16[512,1024]{1,0:T(8,128)(2,1)}, bf16[512,1024]{1,0:T(8,128)(2,1)S(1)}, u32[]{:S(2)}) copy-start(bf16[512,1024]{1,0:T(8,128)(2,1)S(1)} %get-tuple-element.44) | copy-start | bytes 3145732
  645.2 1.4 copy-start.7
  647.9 18.2 %copy-start.12 = (bf16[1024,512]{1,0:T(8,128)(2,1)S(1)}, bf16[1024,512]{1,0:T(8,128)(2,1)}, u32[]{:S(2)}) copy-start(bf16[1024,512]{1,0:T(8,128)(2,1)} %copy-done.11) | copy-start | bytes 3145732
  647.9 18.2 %copy-start.14 = (bf16[1024,512]{1,0:T(8,128)(2,1)S(1)}, bf16[1024,512]{1,0:T(8,128)(2,1)}, u32[]{:S(2)}) copy-start(bf16[1024,512]{1,0:T(8,128)(2,1)} %copy-done.13) | copy-start | bytes 3145732
  723.4 1.6 copy-start.1
  734.4 52.1 %all-to-all-start.4 = ((bf16[1,2,128,32,128]{4,1,2,0,3:T(2,128)(2,1)}), bf16[1,2,128,32,128]{4,1,2,0,3:T(2,128)(2,1)S(1)}, u32[]{:S(2)}, u32[]{:S(2)}) async-start(bf16[1,2,128,32,128]{4,1,2,0,3:T(2,128)(2,1)} %copy.106), calls=%async_computation.4 | async-start | bytes 4194304 | tf_op jit(solution)/shard_map/all_to_all | solution.py:82
  786.5 1.4 copy-start.2
  787.9 52.6 %all-to-all-start.10 = ((bf16[1,2,128,32,128]{4,1,2,0,3:T(2,128)(2,1)}), bf16[1,2,128,32,128]{4,1,2,0,3:T(2,128)(2,1)S(1)}, u32[]{:S(2)}, u32[]{:S(2)}) async-start(bf16[1,2,128,32,128]{4,1,2,0,3:T(2,128)(2,1)} %copy.128), calls=%async_computation.10 | async-start | bytes 4194304 | tf_op jit(solution)/shard_map/all_to_all | solution.py:82
  799.7 4.2 copy-start.10
  840.5 19.4 %all-to-all-start.5 = ((bf16[1,512,4,128]{3,2,0,1:T(4,128)(2,1)}), bf16[1,512,4,128]{3,2,0,1:T(4,128)(2,1)}, u32[]{:S(2)}, u32[]{:S(2)}) async-start(bf16[1,512,4,128]{3,2,0,1:T(4,128)(2,1)} %copy.108), calls=%async_computation.5 | async-start | bytes 1048576 | tf_op jit(solution)/shard_map/all_to_all | solution.py:90
  848.1 60.4 %reduce-scatter.2.cloned.1.call-start = ((), (), s32[]{:S(2)}) async-start(), calls=%async_computation.15 | async-start | bytes 1179648 | tf_op jit(solution)/shard_map/reduce_scatter | solution.py:147
  899.4 1.7 copy-start.8
  899.5 1.8 copy-start.5
  899.5 1.8 copy-start.6
Sparse Core Ops, SparseCore 0:
  9.8 37.0 all-gather.4
  50.1 350.9 all-gather.2
  871.3 37.1 reduce-scatter.1
where the time goes:
time: 929 us; the launch traced here: 917 us
  waiting for transfers between devices  588 us (63%)
  blocking collectives  111 us (12%)
  local copies, waits for them, and re-layouts  65.3 us (7%)
  starting transfers between devices  58.1 us (6%)
  matrix products  42.8 us (5%)
  other arithmetic  37.4 us (4%)
  between operations  14.7 us (2%)
    all_gather x1, waiting for transfers between devices, shards(): gathered_cols = lax.all_gather(out_grad, 'dp', axis=1, tiled=True)  354 us
    all_to_all x3, waiting for transfers between devices, spread_inverse(): lax.all_to_all(turned, 'context', split_axis=3, concat_axis=2, tiled=True)  107 us
    all_to_all x2, waiting for transfers between devices, spread_forward(): lax.all_to_all(turned, 'context', split_axis=2, concat_axis=3, tiled=True)  83.4 us
    all_to_all x1, blocking collectives, spread_forward(): lax.all_to_all(turned, 'context', split_axis=2, concat_axis=3, tiled=True)  51.7 us
    all_to_all x2, blocking collectives, spread_inverse(): lax.all_to_all(values, 'context', split_axis=1, concat_axis=2, tiled=True)  41.6 us
    all_gather x1, waiting for transfers between devices, shards(): weight_rows = lax.all_gather(out_weight, 'context', axis=1, tiled=True)  29.9 us
    another operation x8, other arithmetic  23.4 us
    all_to_all x3, starting transfers between devices, spread_inverse(): lax.all_to_all(turned, 'context', split_axis=3, concat_axis=2, tiled=True)  21.9 us
  transfers between devices with their start and end apart: 11, of which 9 were waited for; matrix products, arithmetic and copies ran while one was open for 8% of the time, Pallas kernels for 0%

commit v1 on v0

v1 whole, which is shorter than its diff:
```python
import functools
import math

import jax
import jax.numpy as jnp
import ml_dtypes
import numpy as np
from jax import lax
from jax.experimental import pallas as pl
from jax.experimental.pallas import tpu as pltpu
from jax.sharding import PartitionSpec as P

CTX = 8
ROWS = 256
STEPS = 64
CH = 16
LEN = 16384
F32 = jnp.float32
BF = jnp.bfloat16
MESH = pl.DeviceIdType.MESH


def tables():
    s = np.arange(STEPS)
    klo = np.arange(STEPS) + 0.25
    th = 2 * np.pi * s[:, None] * klo[None, :] / STEPS
    eye = np.eye(CH)
    fwd = np.concatenate([np.kron(np.cos(th), eye), np.kron(-np.sin(th), eye)], 1)
    b = np.arange(ROWS)
    ph = 2 * np.pi * ((b[:, None] * b[None, :]) % ROWS) / ROWS
    c, sn = np.cos(ph), np.sin(ph)
    tf = np.block([[c, sn], [-sn, c]])
    ps = 2 * np.pi * b[:, None] * klo[None, :] / LEN
    twc = np.repeat(np.cos(ps), CH, axis=1).astype(np.float32)
    tws = np.repeat(np.sin(ps), CH, axis=1).astype(np.float32)
    perm = np.zeros((8, 8, CH, 8, 8, CH), np.float32)
    for a in range(8):
        for g in range(8):
            for k in range(CH):
                perm[a, g, k, g, a, k] = 1
    perm = perm.reshape(1024, 1024)
    low = lambda z: np.ascontiguousarray(z).astype(ml_dtypes.bfloat16)
    return low(perm), low(fwd), low(fwd.T), low(tf), low(tf.T), twc, tws


def kernel(
    proj, taps, grad, weight, perm_h, kf_h, ki_h, tf_h, ti_h, twc_h, tws_h,
    o_streams, o_filter, o_weight,
    qkv, tap, G, W, perm, kf, ki, tf, ti, twc, tws,
    cat, send, recv, spec, wide, up, conv, out_t,
    ps, ps2, pr1, pr2, outs, outf, outw,
    lsem, osem, gs, gr, xs, xr, ws, wr, rs, rr,
):
    me = lax.axis_index("dp")
    ctx = lax.axis_index("context")
    yy, hh, xx = me // 8, (me // 4) % 2, me % 4
    zz, core = ctx // 2, ctx % 2
    sib = ctx + 1 - 2 * core

    def dev(dy, dx, flip):
        h = (1 - hh) if flip else hh
        return (lax.rem(yy + dy + 4, 4) * 2 + h) * 4 + lax.rem(xx + dx + 4, 4)

    loads = {}

    def load(name, src, dst, k):
        loads[name] = pltpu.make_async_copy(src, dst, lsem.at[k])
        loads[name].start()

    load("g", grad, G.at[me], 0)
    load("w", weight, W.at[ctx], 1)
    load("qkv", proj, qkv, 2)
    load("perm", perm_h, perm, 3)
    load("tap", taps, tap, 4)
    load("kf", kf_h, kf, 5)
    load("tf", tf_h, tf, 6)
    load("twc", twc_h, twc, 7)
    load("tws", tws_h, tws, 8)
    load("ki", ki_h, ki, 9)
    load("ti", ti_h, ti, 10)

    bar = pltpu.get_barrier_semaphore()
    for r in range(1, CTX):
        pl.semaphore_signal(bar, inc=1, device_id=(me, lax.rem(ctx + r, CTX)), device_id_type=MESH)
    for d in (dev(0, 1, 0), dev(0, -1, 0), dev(1, 0, 0), dev(-1, 0, 0), dev(0, 0, 1)):
        pl.semaphore_signal(bar, inc=1, device_id=(d, ctx), device_id_type=MESH)
    pl.semaphore_wait(bar, CTX - 1 + 5)

    sent = []

    def remote(src, dst, ssem, rsem, where):
        copy = pltpu.make_async_remote_copy(
            src_ref=src, dst_ref=dst, send_sem=ssem, recv_sem=rsem,
            device_id=where, device_id_type=MESH,
        )
        copy.start()
        sent.append(copy)

    def arrived(buf, rsem):
        pltpu.make_async_remote_copy(
            src_ref=buf, dst_ref=buf, send_sem=gs.at[0], recv_sem=rsem,
            device_id=(me, sib), device_id_type=MESH,
        ).wait_recv()

    nsend = [0]

    def piece(i, lo, n):
        return G.at[i, pl.ds(lo * 512, n * 512)]

    def push(i, lo, n, to):
        k = nsend[0]
        nsend[0] += 1
        p = piece(i, lo, n)
        remote(p, p, gs.at[k], gr.at[i, lo], (to, ctx))

    def got(i, lo, n):
        arrived(piece(i, lo, n), gr.at[i, lo])

    def place(half, u, v, flip):
        return dev(v, u, flip) if half == 0 else dev(u, v, flip)

    def nb(half, axis, step):
        return place(half, step, 0, 0) if axis == 0 else place(half, 0, step, 0)

    def e0(flip):
        src = dev(0, 0, flip)
        for axis in (0, 1):
            for half in (0, 1):
                for step in (1, -1):
                    push(src, 2 * half, 2, nb(half, axis, step))

    def e1(flip):
        for half in (0, 1):
            for u in (-1, 1):
                got(place(half, u, 0, flip), 2 * half, 2)
                q = 2 * half + (0 if u == -1 else 1)
                push(place(half, u, 0, flip), q, 1, nb(half, 0, -u))
        for u in (-1, 1):
            for half in (0, 1):
                for step in (1, -1):
                    push(place(half, u, 0, flip), 2 * half, 2, nb(half, 1, step))

    def e2(flip):
        for q in (0, 1):
            for half in (0, 1):
                i = place(half, 2, 0, flip)
                got(i, 2 * half + q, 1)
                for step in (1, -1):
                    push(i, 2 * half + q, 1, nb(half, 1, step))

    def e3(flip, us):
        for u in us:
            for half in (0, 1):
                for v in (-1, 1):
                    i = place(half, u, v, flip)
                    if u == 2:
                        got(i, 2 * half, 1)
                        got(i, 2 * half + 1, 1)
                    else:
                        got(i, 2 * half, 2)
                    q = 2 * half + (0 if v == -1 else 1)
                    push(i, q, 1, nb(half, 1, -v))

    def e4(flip):
        for u in (0, -1, 1, 2):
            for half in (0, 1):
                i = place(half, u, 2, flip)
                got(i, 2 * half, 1)
                got(i, 2 * half + 1, 1)

    def exchange(sig):
        for r in range(1, CTX):
            to = lax.rem(ctx + r, CTX)
            remote(send.at[sig, to], recv.at[sig, ctx], xs.at[sig, r], xr.at[sig, r], (me, to))
        own = pltpu.make_async_copy(send.at[sig, ctx], recv.at[sig, ctx], xr.at[sig, 0])
        own.start()
        return own

    def exchanged(sig, own):
        own.wait()
        for r in range(1, CTX):
            frm = lax.rem(ctx - r + CTX, CTX)
            arrived(recv.at[sig, frm], xr.at[sig, r])

    def dot(a, b):
        return jnp.dot(a, b, preferred_element_type=F32)

    def chunk(n):
        return pl.ds(pl.multiple_of(n * 256, 256), 256)

    def spread(sig):
        def body(n, _):
            z = dot(cat[...], perm[:, chunk(n)]).astype(BF)
            send[sig, 2 * n] = z[:, :128]
            send[sig, 2 * n + 1] = z[:, 128:]
            return 0
        lax.fori_loop(0, 4, body, 0)

    def gathered(sig):
        for d in range(CTX):
            cat[:, d * 128:(d + 1) * 128] = recv[sig, d]

    def collect(sig, use):
        gathered(sig)

        def body(n, _):
            z = dot(cat[...], perm[:, chunk(n)])
            for k in (0, 1):
                use(pl.ds(pl.multiple_of((2 * n + k) * 256, 256), 256), z[:, k * 128:(k + 1) * 128])
            return 0
        lax.fori_loop(0, 4, body, 0)

    def forward(sig):
        gathered(sig)

        def body(n, _):
            lanes = chunk(n)
            x = cat[...]
            re = dot(x, kf[:, lanes])
            im = dot(x, kf[:, pl.ds(pl.multiple_of(1024 + n * 256, 256), 256)])
            c, s = twc[:, lanes], tws[:, lanes]
            y = jnp.concatenate([(re * c + im * s).astype(BF), (im * c - re * s).astype(BF)], 0)
            spec[sig, :, lanes] = dot(tf[...], y).astype(BF)
            return 0
        lax.fori_loop(0, 4, body, 0)

    def inverse(first, second, conj, sig):
        def body(n, _):
            lanes = chunk(n)
            ar = spec[first, 0:256, lanes].astype(F32)
            ai = spec[first, 256:512, lanes].astype(F32)
            br = spec[second, 0:256, lanes].astype(F32)
            bi = spec[second, 256:512, lanes].astype(F32)
            if conj:
                pr, pi = ar * br + ai * bi, ar * bi - ai * br
            else:
                pr, pi = ar * br - ai * bi, ar * bi + ai * br
            p = jnp.concatenate([pr.astype(BF), pi.astype(BF)], 0)
            v = dot(ti[...], p)
            vr, vi = v[:256], v[256:]
            c, s = twc[:, lanes], tws[:, lanes]
            wide[:, lanes] = (vr * c - vi * s).astype(BF)
            wide[:, pl.ds(pl.multiple_of(1024 + n * 256, 256), 256)] = (vi * c + vr * s).astype(BF)
            return 0
        lax.fori_loop(0, 4, body, 0)

        def last(n, _):
            z = (dot(wide[...], ki[:, chunk(n)]) * (1.0 / LEN)).astype(BF)
            send[sig, 2 * n] = z[:, :128]
            send[sig, 2 * n + 1] = z[:, 128:]
            return 0
        lax.fori_loop(0, 4, last, 0)

    def upstream(flip):
        h = (1 - hh) if flip else hh

        def body(t, _):
            rows = pl.ds(pl.multiple_of(t * 256, 256), 256)
            acc = up[rows, :] if flip else jnp.zeros((256, 128), F32)
            for y in range(4):
                g = y * 2 + h
                x = jnp.concatenate([G[4 * g + k, rows, :] for k in range(4)], 1)
                acc = acc + lax.dot_general(
                    x, W[g], (((1,), (1,)), ((), ())), preferred_element_type=F32
                )
            up[rows, :] = acc
            return 0
        lax.fori_loop(0, 8, body, 0)

    loads["g"].wait()
    e0(0)
    for half in (0, 1):
        push(me, 2 * half, 2, dev(0, 0, 1))
    loads["w"].wait()
    for r in range(1, 4):
        remote(W.at[ctx], W.at[ctx], ws.at[r], wr.at[r], (me, lax.rem(zz + r, 4) * 2 + core))
    remote(W.at[ctx], W.at[ctx], ws.at[4], wr.at[4], (me, sib))
    loads["qkv"].wait()
    loads["perm"].wait()
    for a in range(8):
        rows = slice(a * 256, (a + 1) * 256)
        cat[:, a * 128:(a + 1) * 128] = (qkv[1, rows].astype(F32) * qkv[2, rows].astype(F32)).astype(BF)
    spread(0)
    own0 = exchange(0)
    loads["tap"].wait()
    for a in range(8):
        cat[:, a * 128:(a + 1) * 128] = tap[a * 256:(a + 1) * 256, :]
    spread(1)
    own1 = exchange(1)

    e1(0)
    e2(0)
    e3(0, (0, -1, 1, 2))

    for r in range(1, 4):
        frm = lax.rem(zz - r + 4, 4) * 2 + core
        arrived(W.at[frm], wr.at[r])
        remote(W.at[frm], W.at[frm], ws.at[4 + r], wr.at[4 + r], (me, sib))

    par = dev(0, 0, 1)
    for half in (0, 1):
        got(par, 2 * half, 2)
    e0(1)
    for k in ("kf", "tf", "twc", "tws"):
        loads[k].wait()
    exchanged(0, own0)
    forward(0)
    e1(1)
    exchanged(1, own1)
    forward(1)
    e2(1)
    loads["ki"].wait()
    loads["ti"].wait()
    inverse(1, 0, False, 3)
    own3 = exchange(3)
    e3(1, (0, -1))
    e4(0)
    arrived(W.at[sib], wr.at[4])
    for r in range(1, 4):
        arrived(W.at[lax.rem(zz - r + 4, 4) * 2 + 1 - core], wr.at[4 + r])
    upstream(0)
    e3(1, (1, 2))
    exchanged(3, own3)

    def use_conv(rows, z):
        conv[rows, :] = z.astype(BF)
    collect(3, use_conv)

    def turn(t, _):
        rows = pl.ds(pl.multiple_of(t * 256, 256), 256)
        o = (qkv[0, rows, :].astype(F32) * conv[rows, :].astype(F32)).astype(BF)
        out_t[:, rows] = o.T
        return 0
    lax.fori_loop(0, 8, turn, 0)
    e4(1)

    upstream(1)
    for a in range(8):
        rows = slice(a * 256, (a + 1) * 256)
        cat[:, a * 128:(a + 1) * 128] = (up[rows, :] * qkv[0, rows].astype(F32)).astype(BF)
    spread(2)
    own2 = exchange(2)

    def part(r, _):
        g = jnp.concatenate([G[4 * r + k] for k in range(4)], 1)
        ps[r] = (dot(out_t[...], g) * (1.0 / math.sqrt(LEN))).astype(BF)
        return 0
    lax.fori_loop(0, CTX, part, 0)
    for r in range(4):
        z = lax.rem(zz + r, 4)
        remote(ps.at[2 * z + 1 - core], pr1.at[r], rs.at[r], rr.at[r], (me, sib))
    for r in range(1, 4):
        z = lax.rem(zz + r, 4)
        arrived(pr1.at[r], rr.at[r])
        ps2[r] = (ps[2 * z + core].astype(F32) + pr1[r].astype(F32)).astype(BF)
        remote(ps2.at[r], pr2.at[r], rs.at[3 + r], rr.at[3 + r], (me, 2 * z + core))

    for a in range(8):
        rows = slice(a * 256, (a + 1) * 256)
        outs[0, rows, :] = (up[rows, :] * conv[rows, :].astype(F32)).astype(BF)
    writes = [pltpu.make_async_copy(outs.at[0], o_streams.at[0], osem.at[0])]
    writes[-1].start()

    exchanged(2, own2)
    forward(2)
    inverse(0, 2, True, 4)
    own4 = exchange(4)
    inverse(1, 2, True, 5)
    own5 = exchange(5)

    arrived(pr1.at[0], rr.at[0])
    total = ps[ctx].astype(F32) + pr1[0].astype(F32)
    for r in range(1, 4):
        arrived(pr2.at[r], rr.at[3 + r])
        total = total + pr2[r].astype(F32)
    outw[...] = total
    writes.append(pltpu.make_async_copy(outw, o_weight, osem.at[1]))
    writes[-1].start()

    exchanged(4, own4)

    def use_taps(rows, z):
        outf[rows, :] = z * (1.0 / math.sqrt(LEN))
    collect(4, use_taps)
    writes.append(pltpu.make_async_copy(outf, o_filter, osem.at[2]))
    writes[-1].start()

    exchanged(5, own5)

    def use_mix(rows, z):
        outs[1, rows, :] = (z * qkv[2, rows, :].astype(F32)).astype(BF)
        outs[2, rows, :] = (z * qkv[1, rows, :].astype(F32)).astype(BF)
    collect(5, use_mix)
    writes.append(pltpu.make_async_copy(outs.at[1], o_streams.at[1], osem.at[3]))
    writes[-1].start()
    writes.append(pltpu.make_async_copy(outs.at[2], o_streams.at[2], osem.at[4]))
    writes[-1].start()

    for copy in sent:
        copy.wait_send()
    for copy in writes:
        copy.wait()


def shards(projected, filter_taps, out_grad, out_weight):
    consts = [jnp.asarray(t) for t in tables()]
    vm = pltpu.VMEM
    sem = pltpu.SemaphoreType.DMA
    return pl.pallas_call(
        kernel,
        out_shape=(
            jax.ShapeDtypeStruct((3, 2048, 128), BF),
            jax.ShapeDtypeStruct((2048, 128), F32),
            jax.ShapeDtypeStruct((128, 512), F32),
        ),
        in_specs=[pl.BlockSpec(memory_space=pl.ANY)] * 11,
        out_specs=(pl.BlockSpec(memory_space=pl.ANY),) * 3,
        scratch_shapes=[
            vm((3, 2048, 128), BF),
            vm((2048, 128), BF),
            vm((32, 2048, 128), BF),
            vm((8, 128, 512), BF),
            vm((1024, 1024), BF),
            vm((1024, 2048), BF),
            vm((2048, 1024), BF),
            vm((512, 512), BF),
            vm((512, 512), BF),
            vm((256, 1024), F32),
            vm((256, 1024), F32),
            vm((256, 1024), BF),
            vm((6, 8, 256, 128), BF),
            vm((6, 8, 256, 128), BF),
            vm((3, 512, 1024), BF),
            vm((256, 2048), BF),
            vm((2048, 128), F32),
            vm((2048, 128), BF),
            vm((128, 2048), BF),
            vm((8, 128, 512), BF),
            vm((4, 128, 512), BF),
            vm((4, 128, 512), BF),
            vm((4, 128, 512), BF),
            vm((3, 2048, 128), BF),
            vm((2048, 128), F32),
            vm((128, 512), F32),
            sem((11,)), sem((5,)),
            sem((96,)), sem((32, 4)),
            sem((6, 8)), sem((6, 8)),
            sem((8,)), sem((8,)),
            sem((8,)), sem((8,)),
        ],
        compiler_params=pltpu.CompilerParams(
            collective_id=0, has_side_effects=True, vmem_limit_bytes=60 * 2**20
        ),
    )(projected, filter_taps, out_grad, out_weight, *consts)


def solution(mesh):
    placed = (P(None, "context", "dp"), P("context", "dp"), P("context", "dp"), P("dp", "context"))
    return jax.shard_map(
        shards,
        mesh=mesh,
        in_specs=placed,
        out_specs=(P(None, "context", "dp"), P("context", "dp"), P("dp", "context")),
        check_vma=False,
    )
```

time: 929 us -> 158 us (0.17); the launches traced: 917 us -> 156 us
  waiting for transfers between devices: 588 us -> 0 us
  Pallas kernels: 0 us -> 150 us
  blocking collectives: 111 us -> 0 us
  local copies, waits for them, and re-layouts: 65.3 us -> 4.43 us
  starting transfers between devices: 58.1 us -> 0 us
  matrix products: 42.8 us -> 0 us
  other arithmetic: 37.4 us -> 0 us
  between operations: 14.7 us -> 0.66 us
    all_gather x2 -> x0, waiting for transfers between devices: 384 us -> none  [the longest x1 354 us: shards(): gathered_cols = lax.all_gather(out_grad, 'dp', axis=1, tiled=True)]
    all_to_all x8 -> x0, waiting for transfers between devices: 196 us -> none  [the longest x3 107 us: spread_inverse(): lax.all_to_all(turned, 'context', split_axis=3, concat_axis=2, tiled=True)]
    pallas_call x0 -> x1, Pallas kernels: none -> 150 us  [shards(): pl.pallas_call(kernel, out_shape=(jax.ShapeDtypeStruct((3, 2048, 128), BF...]
    all_to_all x4 -> x0, blocking collectives: 111 us -> none  [the longest x1 51.7 us: spread_forward(): lax.all_to_all(turned, 'context', split_axis=2, concat_axis=3, tiled=True)]
    all_to_all x8 -> x0, starting transfers between devices: 57.7 us -> none  [the longest x3 21.9 us: spread_inverse(): lax.all_to_all(turned, 'context', split_axis=3, concat_axis=2, tiled=True)]
    dot_general x14 -> x0, matrix products: 42.8 us -> none  [the longest x1 11.6 us: shards(): lax.dot_general(gathered_cols, weight_rows, (((1,), (1,)), ((), ())), pre...]
    another operation x22 -> x0, other arithmetic: 35 us -> none
    another operation x11 -> x0, local copies, waits for them, and re-layouts: 32.4 us -> none
  transfers between devices with their start and end apart: 11 -> 0, of which waited for: 9 -> 0; matrix products, arithmetic and copies ran while one was open for 8% -> 0% of each run, Pallas kernels for 0% -> 0%
where the time goes in v1:
time: 158 us; the launch traced here: 156 us
  Pallas kernels  150 us (95%)
  local copies, waits for them, and re-layouts  4.43 us (3%)
    pallas_call x1, Pallas kernels, shards(): pl.pallas_call(kernel, out_shape=(jax.ShapeDtypeStruct((3, 2048, 128), BF...  150 us
    unnamed x7, local copies, waits for them, and re-layouts  4.43 us

profile of v1, /device:TPU:41, one launch (start us, length us, event | category | flops | bytes accessed | tf_op | source)
XLA Modules:
  0.0 155.5 jit_solution(13809492673239151990)
XLA Ops:
  0.6 150.4 %shard_map.130 = (bf16[3,2048,128]{2,1,0:T(8,128)(2,1)}, f32[2048,128]{1,0:T(8,128)}, f32[128,512]{1,0:T(8,128)}) custom-call(bf16[3,2048,128]{2,1,0:T(8,128)(2,1)} %proj.1, bf16[2048,128]{1,0:T(8,128)(2,1)} %taps.1, bf16[2048,128]{1,0:T(8,128)(2,1)} %grad.1, bf16[128,512]{1,0:T(8,128)(2,1)} %weight.1, bf16[1024,1024]{1,0:T(8,128)(2,1)} %constant.14.clone.perm_h, ...), custom_call_target="tpu_custom_call" | custom-call | tf_op jit(solution)/shard_map/pallas_call | solution.py:409
  151.1 0.0 copy-start
  151.1 0.0 copy-start.1
  151.1 2.8 %copy.17 = bf16[3,2048,128]{2,1,0:T(8,128)(2,1)} copy(bf16[3,2048,128]{2,1,0:T(8,128)(2,1)} %get-tuple-element.6) | data formatting | bytes 3145728
  153.9 0.0 copy-done
  153.9 1.0 copy.18
  154.8 0.0 copy-done.1
  154.8 0.7 copy.19
Async XLA Ops:
  151.1 2.8 %copy-start = (f32[2048,128]{1,0:T(8,128)S(1)}, f32[2048,128]{1,0:T(8,128)}, u32[]{:S(2)}) copy-start(f32[2048,128]{1,0:T(8,128)} %get-tuple-element.7) | copy-start | bytes 3145732
  151.1 3.7 %copy-start.1 = (f32[128,512]{1,0:T(8,128)S(1)}, f32[128,512]{1,0:T(8,128)}, u32[]{:S(2)}) copy-start(f32[128,512]{1,0:T(8,128)} %get-tuple-element.8) | copy-start | bytes 786436

commit v2 on v1

v2 whole, which is shorter than its diff:
```python
import functools
import math

import jax
import jax.numpy as jnp
import ml_dtypes
import numpy as np
from jax import lax
from jax.experimental import pallas as pl
from jax.experimental.pallas import tpu as pltpu
from jax.sharding import PartitionSpec as P

CTX = 8
ROWS = 256
STEPS = 64
CH = 16
LEN = 16384
F32 = jnp.float32
BF = jnp.bfloat16
MESH = pl.DeviceIdType.MESH
ALL = pl.ds(0, ROWS)
PASSES = ((0, 256), (0, 192), (192, 64))
PACE = 3


def tables():
    s = np.arange(STEPS)
    klo = np.arange(STEPS) + 0.25
    th = 2 * np.pi * s[:, None] * klo[None, :] / STEPS
    eye = np.eye(CH)
    fwd = np.concatenate([np.kron(np.cos(th), eye), np.kron(-np.sin(th), eye)], 1)
    b = np.arange(ROWS)
    ph = 2 * np.pi * ((b[:, None] * b[None, :]) % ROWS) / ROWS
    c, sn = np.cos(ph), np.sin(ph)
    tf = np.block([[c, sn], [-sn, c]])
    ps = 2 * np.pi * b[:, None] * klo[None, :] / LEN
    twc = np.repeat(np.cos(ps), CH, axis=1).astype(np.float32)
    tws = np.repeat(np.sin(ps), CH, axis=1).astype(np.float32)
    perm = np.zeros((8, 8, CH, 8, 8, CH), np.float32)
    for a in range(8):
        for g in range(8):
            for k in range(CH):
                perm[a, g, k, g, a, k] = 1
    perm = perm.reshape(1024, 1024)
    low = lambda z: np.ascontiguousarray(z).astype(ml_dtypes.bfloat16)
    return low(perm), low(fwd), low(fwd.T), low(tf), low(tf.T), twc, tws


def kernel(
    proj, taps, grad, weight, perm_h, kf_h, ki_h, tf_h, ti_h, twc_h, tws_h,
    o_streams, o_weight,
    qkv, tap, G, W, wt, perm, kf, ki, tf, ti, twc, tws,
    cat, send, recv, spec, turned, wide, up, conv, out_t,
    ps, psf, ps2, pr1, pr2, outs, outw,
    lsem, osem, gs, gr, xs, xr, ws, wr, rs, rr,
):
    me = lax.axis_index("dp")
    ctx = lax.axis_index("context")
    yy, hh, xx = me // 8, (me // 4) % 2, me % 4
    zz, core = ctx // 2, ctx % 2
    sib = ctx + 1 - 2 * core

    def dev(dy, dx, flip):
        h = (1 - hh) if flip else hh
        return (lax.rem(yy + dy + 4, 4) * 2 + h) * 4 + lax.rem(xx + dx + 4, 4)

    def chip(r):
        return lax.rem(zz + r + 4, 4)

    loads = {}

    def load(name, src, dst, k):
        loads[name] = pltpu.make_async_copy(src, dst, lsem.at[k])
        loads[name].start()

    load("g", grad, G.at[me], 0)
    load("qkv", proj, qkv, 2)
    load("perm", perm_h, perm, 3)
    load("tap", taps, tap, 4)
    load("w", weight, W.at[ctx], 1)
    load("kf", kf_h, kf, 5)
    load("tf", tf_h, tf, 6)
    load("twc", twc_h, twc, 7)
    load("tws", tws_h, tws, 8)
    load("ki", ki_h, ki, 9)
    load("ti", ti_h, ti, 10)

    bar = pltpu.get_barrier_semaphore()
    for r in range(1, CTX):
        pl.semaphore_signal(bar, inc=1, device_id=(me, lax.rem(ctx + r, CTX)), device_id_type=MESH)
    for d in (dev(0, 1, 0), dev(0, -1, 0), dev(1, 0, 0), dev(-1, 0, 0), dev(0, 0, 1)):
        pl.semaphore_signal(bar, inc=1, device_id=(d, ctx), device_id_type=MESH)
    pl.semaphore_wait(bar, CTX - 1 + 5)

    sent = []

    def remote(src, dst, ssem, rsem, where):
        copy = pltpu.make_async_remote_copy(
            src_ref=src, dst_ref=dst, send_sem=ssem, recv_sem=rsem,
            device_id=where, device_id_type=MESH,
        )
        copy.start()
        sent.append(copy)

    def arrived(buf, rsem):
        pltpu.make_async_remote_copy(
            src_ref=buf, dst_ref=buf, send_sem=gs.at[0], recv_sem=rsem,
            device_id=(me, sib), device_id_type=MESH,
        ).wait_recv()

    nsend = [0]
    todo = []

    def flush():
        while todo:
            todo.pop(0)()

    def piece(i, p, q, n):
        b0, nb = PASSES[p]
        return G.at[i, :, pl.ds(b0 + q * (nb // 4), n * (nb // 4)), :]

    def push(i, p, q, n, to):
        k = nsend[0]
        nsend[0] += 1
        r = piece(i, p, q, n)
        remote(r, r, gs.at[k], gr.at[i, 4 * (p // 2) + q], (to, ctx))
        if todo and k % PACE == PACE - 1:
            todo.pop(0)()

    def got(i, p, q, n):
        arrived(piece(i, p, q, n), gr.at[i, 4 * (p // 2) + q])

    def place(half, u, v, flip):
        return dev(v, u, flip) if half == 0 else dev(u, v, flip)

    def nb(half, axis, step):
        return place(half, step, 0, 0) if axis == 0 else place(half, 0, step, 0)

    def e0(p):
        flip = p > 0
        src = dev(0, 0, flip)
        for axis in (0, 1):
            for half in (0, 1):
                for step in (1, -1):
                    push(src, p, 2 * half, 2, nb(half, axis, step))

    def e1(p):
        flip = p > 0
        for half in (0, 1):
            for u in (-1, 1):
                i = place(half, u, 0, flip)
                got(i, p, 2 * half, 2)
                push(i, p, 2 * half + (0 if u == -1 else 1), 1, nb(half, 0, -u))
        for u in (-1, 1):
            for half in (0, 1):
                for step in (1, -1):
                    push(place(half, u, 0, flip), p, 2 * half, 2, nb(half, 1, step))

    def e2(p):
        flip = p > 0
        for q in (0, 1):
            for half in (0, 1):
                i = place(half, 2, 0, flip)
                got(i, p, 2 * half + q, 1)
                for step in (1, -1):
                    push(i, p, 2 * half + q, 1, nb(half, 1, step))

    def e3(p, us=(0, -1, 1, 2)):
        flip = p > 0
        for u in us:
            for half in (0, 1):
                for v in (-1, 1):
                    i = place(half, u, v, flip)
                    if u == 2:
                        got(i, p, 2 * half, 1)
                        got(i, p, 2 * half + 1, 1)
                    else:
                        got(i, p, 2 * half, 2)
                    push(i, p, 2 * half + (0 if v == -1 else 1), 1, nb(half, 1, -v))

    def e4(p):
        flip = p > 0
        for u in (0, -1, 1, 2):
            for half in (0, 1):
                i = place(half, u, 2, flip)
                got(i, p, 2 * half, 1)
                got(i, p, 2 * half + 1, 1)

    def swap(p):
        for half in (0, 1):
            push(me, p, 2 * half, 2, dev(0, 0, 1))

    def swapped(p):
        for half in (0, 1):
            got(dev(0, 0, 1), p, 2 * half, 2)

    owns = {}

    def ship(sig, slot, r, rows):
        n = chip(r)
        for k in (0, 1):
            to = 2 * n + (core if k == 0 else 1 - core)
            src, dst = send.at[sig, to, rows], recv.at[sig, ctx, rows]
            if r == 0 and k == 0:
                owns[slot] = pltpu.make_async_copy(src, dst, xr.at[slot, 0])
                owns[slot].start()
            else:
                remote(src, dst, xs.at[slot, 2 * r + k], xr.at[slot, 2 * r + k], (me, to))

    def exchanged(sig, slot, rows):
        owns[slot].wait()
        for r in range(4):
            for k in (0, 1):
                if r or k:
                    frm = 2 * chip(-r) + (core if k == 0 else 1 - core)
                    arrived(recv.at[sig, frm, rows], xr.at[slot, 2 * r + k])

    def dot(a, b):
        return jnp.dot(a, b, preferred_element_type=F32)

    def chunk(n):
        return pl.ds(pl.multiple_of(n * 256, 256), 256)

    def deliver(sig, slot, rows, make, at_once):
        for r in (2, 1, 3, 0):
            n = chip(r)
            z = make(chunk(n))
            send[sig, 2 * n, rows] = z[:, :128]
            send[sig, 2 * n + 1, rows] = z[:, 128:]
            go = functools.partial(ship, sig, slot, r, rows)
            if at_once:
                go()
            else:
                todo.append(go)

    def spread(sig, slot, rows, at_once=False):
        deliver(sig, slot, rows, lambda lanes: dot(cat[rows, :], perm[:, lanes]).astype(BF), at_once)

    def gathered(sig, rows):
        for d in range(CTX):
            cat[rows, d * 128:(d + 1) * 128] = recv[sig, d, rows]

    def collect(sig, use):
        gathered(sig, ALL)

        def body(n, _):
            z = dot(cat[...], perm[:, chunk(n)])
            use(2 * n, z[:, :128])
            use(2 * n + 1, z[:, 128:])
            return 0
        lax.fori_loop(0, 4, body, 0)

    def first_stage(sig, b0, nb):
        rows = pl.ds(b0, nb)
        gathered(sig, rows)

        def body(n, _):
            lanes = chunk(n)
            x = cat[rows, :]
            re = dot(x, kf[:, lanes])
            im = dot(x, kf[:, pl.ds(pl.multiple_of(1024 + n * 256, 256), 256)])
            c, s = twc[rows, lanes], tws[rows, lanes]
            turned[rows, lanes] = (re * c + im * s).astype(BF)
            turned[pl.ds(256 + b0, nb), lanes] = (im * c - re * s).astype(BF)
            return 0
        lax.fori_loop(0, 4, body, 0)

    def second_stage(sig):
        def body(n, _):
            lanes = chunk(n)
            spec[sig, :, lanes] = dot(tf[...], turned[:, lanes]).astype(BF)
            return 0
        lax.fori_loop(0, 4, body, 0)

    def inverse(first, second, conj, sig, at_once):
        def body(n, _):
            lanes = chunk(n)
            ar = spec[first, 0:256, lanes].astype(F32)
            ai = spec[first, 256:512, lanes].astype(F32)
            br = spec[second, 0:256, lanes].astype(F32)
            bi = spec[second, 256:512, lanes].astype(F32)
            if conj:
                pr, pi = ar * br + ai * bi, ar * bi - ai * br
            else:
                pr, pi = ar * br - ai * bi, ar * bi + ai * br
            p = jnp.concatenate([pr.astype(BF), pi.astype(BF)], 0)
            v = dot(ti[...], p)
            vr, vi = v[:256], v[256:]
            c, s = twc[:, lanes], tws[:, lanes]
            wide[:, lanes] = (vr * c - vi * s).astype(BF)
            wide[:, pl.ds(pl.multiple_of(1024 + n * 256, 256), 256)] = (vi * c + vr * s).astype(BF)
            return 0
        lax.fori_loop(0, 4, body, 0)
        deliver(
            sig, sig, ALL,
            lambda lanes: (dot(wide[...], ki[:, lanes]) * (1.0 / LEN)).astype(BF), at_once,
        )

    def upstream(p, lo=0, hi=8):
        flip = p > 0
        h = (1 - hh) if flip else hh
        b0, nb = PASSES[p]
        na = 256 // nb if nb < 256 else 1
        rows = pl.ds(b0, nb)

        def body(t, _):
            at = pl.ds(t * na, na)
            acc = up[at, rows, :].reshape(na * nb, 128) if flip else jnp.zeros((na * nb, 128), F32)
            for y in range(4):
                g = y * 2 + h
                x = jnp.concatenate(
                    [G[4 * g + k, at, rows, :].reshape(na * nb, 128) for k in range(4)], 1
                )
                acc = acc + dot(x, wt[g])
            up[at, rows, :] = acc.reshape(na, nb, 128)
            return 0
        lax.fori_loop(lo // na, hi // na, body, 0)

    def gate(p, slot, at_once):
        b0, nb = PASSES[p]
        rows = pl.ds(b0, nb)
        for a in range(8):
            cat[rows, a * 128:(a + 1) * 128] = (up[a, rows] * qkv[0, a, rows].astype(F32)).astype(BF)
        spread(2, slot, rows, at_once)

    def move(src, dst, k, to):
        pltpu.make_async_remote_copy(
            src_ref=src, dst_ref=dst, send_sem=rs.at[k], recv_sem=rr.at[k],
            device_id=(me, to), device_id_type=MESH,
        ).start()

    def half_part(r, b):
        g = jnp.concatenate(
            [G[4 * r + k, :, b:b + 128, :].reshape(1024, 128) for k in range(4)], 1
        )
        o = jnp.concatenate([out_t[:, a * 256 + b:a * 256 + b + 128] for a in range(8)], 1)
        return dot(o, g)

    def part_first():
        def body(y, _):
            psf[y] = half_part(2 * y + 1 - hh, 0)
            return 0
        lax.fori_loop(0, 4, body, 0)

    def part(flip):
        h = (1 - hh) if flip else hh

        def body(y, _):
            r = 2 * y + h
            if flip:
                z = psf[y] + half_part(r, 128)
            else:
                g = jnp.concatenate([G[4 * r + k].reshape(2048, 128) for k in range(4)], 1)
                z = dot(out_t[...], g)
            ps[r] = (z * (1.0 / math.sqrt(LEN))).astype(BF)
            return 0
        lax.fori_loop(0, 4, body, 0)

        @pl.when(core != h)
        def _():
            for r in (2, 1, 3, 0):
                move(ps.at[2 * chip(r) + h], pr1.at[r], r, sib)

    def combine(flip):
        h = (1 - hh) if flip else hh

        @pl.when(core == h)
        def _():
            for r in (2, 1, 3):
                arrived(pr1.at[r], rr.at[r])
                n = 2 * chip(r) + h
                ps2[r] = (ps[n].astype(F32) + pr1[r].astype(F32)).astype(BF)
                move(ps2.at[r], pr2.at[r], 3 + r, n)

    def weights_go(s):
        if s == 0:
            remote(W.at[ctx], W.at[ctx], ws.at[4], wr.at[4], (me, sib))
            for r in (2, 1, 3):
                todo.append(functools.partial(
                    remote, W.at[ctx], W.at[ctx], ws.at[r], wr.at[r], (me, 2 * chip(r) + core)
                ))
        if s == 2:
            for r in range(1, 4):
                frm = 2 * chip(-r) + core
                arrived(W.at[frm], wr.at[r])
                remote(W.at[frm], W.at[frm], ws.at[4 + r], wr.at[4 + r], (me, sib))

    def weights_in():
        arrived(W.at[sib], wr.at[4])
        for r in range(1, 4):
            arrived(W.at[2 * chip(-r) + 1 - core], wr.at[4 + r])

        def body(g, _):
            wt[g] = W[g].T
            return 0
        lax.fori_loop(0, CTX, body, 0)

    def use_conv(a, z):
        conv[a] = z.astype(BF)

    def turn(a, _):
        o = (qkv[0, a].astype(F32) * conv[a].astype(F32)).astype(BF)
        out_t[:, chunk(a)] = o.T
        return 0

    _, rows0, rows1 = (pl.ds(*q) for q in PASSES)

    loads["g"].wait()
    e0(0)
    swap(1)
    loads["qkv"].wait()
    loads["perm"].wait()
    for a in range(8):
        cat[:, a * 128:(a + 1) * 128] = (qkv[1, a].astype(F32) * qkv[2, a].astype(F32)).astype(BF)
    spread(0, 0, ALL)
    loads["tap"].wait()
    for a in range(8):
        cat[:, a * 128:(a + 1) * 128] = tap[a]
    spread(1, 1, ALL)
    todo.append(functools.partial(swap, 2))
    loads["w"].wait()
    weights_go(0)
    e1(0)
    e2(0)
    e3(0, (0,))
    for k in ("kf", "tf", "twc", "tws", "ki", "ti"):
        loads[k].wait()
    e3(0, (-1, 1))
    e3(0, (2,))
    flush()
    swapped(1)
    e0(1)
    swapped(2)
    e0(2)
    e4(0)
    exchanged(0, 0, ALL)
    first_stage(0, 0, 256)
    second_stage(0)
    e1(1)
    exchanged(1, 1, ALL)
    first_stage(1, 0, 256)
    second_stage(1)
    e2(1)
    inverse(1, 0, False, 3, False)
    e3(1, (0,))
    weights_go(2)
    e1(2)
    e3(1, (-1, 1))
    weights_in()
    upstream(0, 0, 4)
    e3(1, (2,))
    upstream(0, 4, 8)
    flush()
    e2(2)
    exchanged(3, 3, ALL)
    collect(3, use_conv)
    lax.fori_loop(0, 8, turn, 0)
    part(0)
    combine(0)
    e4(1)
    upstream(1)
    gate(1, 2, False)
    e3(2)
    flush()
    part_first()
    e4(2)
    upstream(2)
    gate(2, 6, True)
    part(1)
    combine(1)
    exchanged(2, 2, rows0)
    first_stage(2, *PASSES[1])

    exchanged(2, 6, rows1)
    first_stage(2, *PASSES[2])
    second_stage(2)
    early = list(sent)
    inverse(0, 2, True, 4, True)
    inverse(1, 2, True, 5, True)

    for a in range(8):
        outs[0, a] = (up[a] * conv[a].astype(F32)).astype(BF)
    writes = [pltpu.make_async_copy(outs.at[0], o_streams.at[0], osem.at[0])]
    writes[-1].start()

    arrived(pr1.at[0], rr.at[0])
    total = ps[ctx].astype(F32) + pr1[0].astype(F32)
    for r in range(1, 4):
        arrived(pr2.at[r], rr.at[3 + r])
        total = total + pr2[r].astype(F32)
    outw[...] = total
    writes.append(pltpu.make_async_copy(outw, o_weight, osem.at[1]))
    writes[-1].start()

    for copy in early:
        copy.wait_send()
    exchanged(4, 4, ALL)

    def use_taps(a, z):
        outs[1, a] = z.astype(BF)
    collect(4, use_taps)
    writes.append(pltpu.make_async_copy(outs.at[1], o_streams.at[1], osem.at[2]))
    writes[-1].start()

    exchanged(5, 5, ALL)

    def use_mix(a, z):
        outs[2, a] = z.astype(BF)
    collect(5, use_mix)
    writes.append(pltpu.make_async_copy(outs.at[2], o_streams.at[2], osem.at[3]))
    writes[-1].start()

    for copy in sent[len(early):]:
        copy.wait_send()
    for k in range(7):
        pltpu.make_async_remote_copy(
            src_ref=ps.at[0], dst_ref=pr1.at[0], send_sem=rs.at[k], recv_sem=rr.at[k],
            device_id=(me, sib), device_id_type=MESH,
        ).wait_send()
    for copy in writes:
        copy.wait()


def finish(found, key, value, weights, o_streams, o_filter, o_weight):
    o_streams[0] = found[0]
    o_filter[...] = found[1].astype(F32) * (1.0 / math.sqrt(LEN))
    mix = found[2].astype(F32)
    o_streams[1] = (mix * value[0].astype(F32)).astype(BF)
    o_streams[2] = (mix * key[0].astype(F32)).astype(BF)
    o_weight[...] = weights[...]


def shards(projected, filter_taps, out_grad, out_weight):
    consts = [jnp.asarray(t) for t in tables()]
    vm = pltpu.VMEM
    sem = pltpu.SemaphoreType.DMA
    found, weights = pl.pallas_call(
        kernel,
        out_shape=(
            jax.ShapeDtypeStruct((3, 8, 256, 128), BF),
            jax.ShapeDtypeStruct((128, 512), F32),
        ),
        in_specs=[pl.BlockSpec(memory_space=pl.ANY)] * 11,
        out_specs=(pl.BlockSpec(memory_space=pl.ANY),) * 2,
        scratch_shapes=[
            vm((3, 8, 256, 128), BF),
            vm((8, 256, 128), BF),
            vm((32, 8, 256, 128), BF),
            vm((8, 128, 512), BF),
            vm((8, 512, 128), BF),
            vm((1024, 1024), BF),
            vm((1024, 2048), BF),
            vm((2048, 1024), BF),
            vm((512, 512), BF),
            vm((512, 512), BF),
            vm((256, 1024), F32),
            vm((256, 1024), F32),
            vm((256, 1024), BF),
            vm((6, 8, 256, 128), BF),
            vm((6, 8, 256, 128), BF),
            vm((3, 512, 1024), BF),
            vm((512, 1024), BF),
            vm((256, 2048), BF),
            vm((8, 256, 128), F32),
            vm((8, 256, 128), BF),
            vm((128, 2048), BF),
            vm((8, 128, 512), BF),
            vm((4, 128, 512), F32),
            vm((4, 128, 512), BF),
            vm((4, 128, 512), BF),
            vm((4, 128, 512), BF),
            vm((3, 8, 256, 128), BF),
            vm((128, 512), F32),
            sem((11,)), sem((5,)),
            sem((184,)), sem((32, 8)),
            sem((7, 8)), sem((7, 8)),
            sem((13,)), sem((8,)),
            sem((8,)), sem((8,)),
        ],
        compiler_params=pltpu.CompilerParams(
            collective_id=0, has_side_effects=True, vmem_limit_bytes=60 * 2**20
        ),
    )(
        projected.reshape(3, 8, 256, 128), filter_taps.reshape(8, 256, 128),
        out_grad.reshape(8, 256, 128), out_weight, *consts,
    )
    rows = pl.BlockSpec((3, 1024, 128), lambda i: (0, i, 0))
    keys = pl.BlockSpec((1, 1024, 128), lambda i: (1, i, 0))
    values = pl.BlockSpec((1, 1024, 128), lambda i: (2, i, 0))
    part = pl.BlockSpec((64, 512), lambda i: (i, 0))
    return pl.pallas_call(
        finish,
        grid=(2,),
        out_shape=(
            jax.ShapeDtypeStruct((3, 2048, 128), BF),
            jax.ShapeDtypeStruct((2048, 128), F32),
            jax.ShapeDtypeStruct((128, 512), F32),
        ),
        in_specs=[rows, keys, values, part],
        out_specs=(rows, pl.BlockSpec((1024, 128), lambda i: (i, 0)), part),
    )(found.reshape(3, 2048, 128), projected, projected, weights)


def solution(mesh):
    placed = (P(None, "context", "dp"), P("context", "dp"), P("context", "dp"), P("dp", "context"))
    return jax.shard_map(
        shards,
        mesh=mesh,
        in_specs=placed,
        out_specs=(P(None, "context", "dp"), P("context", "dp"), P("dp", "context")),
        check_vma=False,
    )
```

time: 158 us -> 149 us (0.943)
  local copies, waits for them, and re-layouts: 4.43 us -> 0 us
  Pallas kernels: 150 us -> 146 us
    pallas_call x1 -> x2, Pallas kernels: 150 us -> 146 us  [the longest x1 143 us: shards(): pl.pallas_call(kernel, out_shape=(jax.ShapeDtypeStruct((3, 8, 256, 128),...]
    unnamed x7 -> x0, local copies, waits for them, and re-layouts: 4.43 us -> none
where the time goes in v2:
time: 149 us; the launch traced here: 147 us
  Pallas kernels  146 us (98%)
    pallas_call x1, Pallas kernels, shards(): pl.pallas_call(kernel, out_shape=(jax.ShapeDtypeStruct((3, 8, 256, 128),...  143 us
    pallas_call x1, Pallas kernels, shards(): pl.pallas_call(finish, grid=(2,), out_shape=(jax.ShapeDtypeStruct((3, 204...  3.06 us

profile of v2, /device:TPU:41, one launch (start us, length us, event | category | flops | bytes accessed | tf_op | source)
XLA Modules:
  0.0 146.6 jit_solution(10836036484881139168)
XLA Ops:
  0.6 142.9 %shard_map.130 = (bf16[3,8,256,128]{3,2,1,0:T(8,128)(2,1)}, f32[128,512]{1,0:T(8,128)}) custom-call(bf16[3,8,256,128]{3,2,1,0:T(8,128)(2,1)} %bitcast.4, bf16[8,256,128]{2,1,0:T(8,128)(2,1)} %bitcast.6, bf16[8,256,128]{2,1,0:T(8,128)(2,1)} %bitcast.7, bf16[128,512]{1,0:T(8,128)(2,1)} %weight.1, bf16[1024,1024]{1,0:T(8,128)(2,1)} %constant.14.clone.perm_h, ...), custom_call_target="tpu_custom_call" | custom-call | tf_op jit(solution)/shard_map/pallas_call | solution.py:537
  143.6 3.1 %shard_map.131 = (bf16[3,2048,128]{2,1,0:T(8,128)(2,1)}, f32[2048,128]{1,0:T(8,128)}, f32[128,512]{1,0:T(8,128)}) custom-call(bf16[3,2048,128]{2,1,0:T(8,128)(2,1)} %bitcast.5, bf16[3,2048,128]{2,1,0:T(8,128)(2,1)} %value.1, bf16[3,2048,128]{2,1,0:T(8,128)(2,1)} %value.1, f32[128,512]{1,0:T(8,128)} %get-tuple-element.6.weights), custom_call_target="tpu_custom_call" | custom-call | tf_op jit(solution)/shard_map/pallas_call | solution.py:591

commit v3 on v2

--- a/solution.py
+++ b/solution.py
@@ -19,7 +19,7 @@
 BF = jnp.bfloat16
 MESH = pl.DeviceIdType.MESH
 ALL = pl.ds(0, ROWS)
-PASSES = ((0, 256), (0, 192), (192, 64))
+PASSES = ((0, 256), (0, 128), (128, 64), (192, 64))
 PACE = 3
 
 
@@ -123,12 +123,12 @@
         k = nsend[0]
         nsend[0] += 1
         r = piece(i, p, q, n)
-        remote(r, r, gs.at[k], gr.at[i, 4 * (p // 2) + q], (to, ctx))
+        remote(r, r, gs.at[k], gr.at[i, 4 * max(p - 1, 0) + q], (to, ctx))
         if todo and k % PACE == PACE - 1:
             todo.pop(0)()
 
     def got(i, p, q, n):
-        arrived(piece(i, p, q, n), gr.at[i, 4 * (p // 2) + q])
+        arrived(piece(i, p, q, n), gr.at[i, 4 * max(p - 1, 0) + q])
 
     def place(half, u, v, flip):
         return dev(v, u, flip) if half == 0 else dev(u, v, flip)
@@ -403,11 +403,13 @@
         out_t[:, chunk(a)] = o.T
         return 0
 
-    _, rows0, rows1 = (pl.ds(*q) for q in PASSES)
+    _, rows0, rows1, rows2 = (pl.ds(*q) for q in PASSES)
 
     loads["g"].wait()
     e0(0)
     swap(1)
+    swap(2)
+    swap(3)
     loads["qkv"].wait()
     loads["perm"].wait()
     for a in range(8):
@@ -417,7 +419,6 @@
     for a in range(8):
         cat[:, a * 128:(a + 1) * 128] = tap[a]
     spread(1, 1, ALL)
-    todo.append(functools.partial(swap, 2))
     loads["w"].wait()
     weights_go(0)
     e1(0)
@@ -430,13 +431,13 @@
     flush()
     swapped(1)
     e0(1)
-    swapped(2)
-    e0(2)
     e4(0)
     exchanged(0, 0, ALL)
     first_stage(0, 0, 256)
     second_stage(0)
     e1(1)
+    swapped(2)
+    e0(2)
     exchanged(1, 1, ALL)
     first_stage(1, 0, 256)
     second_stage(1)
@@ -444,6 +445,8 @@
     inverse(1, 0, False, 3, False)
     e3(1, (0,))
     weights_go(2)
+    swapped(3)
+    e0(3)
     e1(2)
     e3(1, (-1, 1))
     weights_in()
@@ -452,6 +455,7 @@
     upstream(0, 4, 8)
     flush()
     e2(2)
+    e1(3)
     exchanged(3, 3, ALL)
     collect(3, use_conv)
     lax.fori_loop(0, 8, turn, 0)
@@ -461,18 +465,26 @@
     upstream(1)
     gate(1, 2, False)
     e3(2)
+    e2(3)
+    flush()
+    e4(2)
+    upstream(2)
+    gate(2, 6, False)
+    e3(3)
     flush()
     part_first()
-    e4(2)
-    upstream(2)
-    gate(2, 6, True)
+    exchanged(2, 2, rows0)
+    first_stage(2, *PASSES[1])
+    e4(3)
+    upstream(3)
+    gate(3, 7, True)
     part(1)
     combine(1)
-    exchanged(2, 2, rows0)
-    first_stage(2, *PASSES[1])
-
     exchanged(2, 6, rows1)
     first_stage(2, *PASSES[2])
+
+    exchanged(2, 7, rows2)
+    first_stage(2, *PASSES[3])
     second_stage(2)
     early = list(sent)
     inverse(0, 2, True, 4, True)
@@ -572,8 +584,8 @@
             vm((3, 8, 256, 128), BF),
             vm((128, 512), F32),
             sem((11,)), sem((5,)),
-            sem((184,)), sem((32, 8)),
-            sem((7, 8)), sem((7, 8)),
+            sem((184,)), sem((32, 12)),
+            sem((8, 8)), sem((8, 8)),
             sem((13,)), sem((8,)),
             sem((8,)), sem((8,)),
         ],

time: 149 us -> 147 us (0.987); the launches traced: 147 us -> 147 us
  no operation moved by 1% of the time
where the time goes in v3:
time: 147 us
  Pallas kernels  147 us (100%)
    pallas_call x1, Pallas kernels, shards(): pl.pallas_call(kernel, out_shape=(jax.ShapeDtypeStruct((3, 8, 256, 128),...  144 us
    pallas_call x1, Pallas kernels, shards(): pl.pallas_call(finish, grid=(2,), out_shape=(jax.ShapeDtypeStruct((3, 204...  3.06 us

profile of v3, /device:TPU:41, one launch (start us, length us, event | category | flops | bytes accessed | tf_op | source)
XLA Modules:
  0.0 147.3 jit_solution(15168563847781110260)
XLA Ops:
  0.6 143.6 %shard_map.130 = (bf16[3,8,256,128]{3,2,1,0:T(8,128)(2,1)}, f32[128,512]{1,0:T(8,128)}) custom-call(bf16[3,8,256,128]{3,2,1,0:T(8,128)(2,1)} %bitcast.4, bf16[8,256,128]{2,1,0:T(8,128)(2,1)} %bitcast.6, bf16[8,256,128]{2,1,0:T(8,128)(2,1)} %bitcast.7, bf16[128,512]{1,0:T(8,128)(2,1)} %weight.1, bf16[1024,1024]{1,0:T(8,128)(2,1)} %constant.14.clone.perm_h, ...), custom_call_target="tpu_custom_call" | custom-call | tf_op jit(solution)/shard_map/pallas_call | solution.py:549
  144.2 3.1 %shard_map.131 = (bf16[3,2048,128]{2,1,0:T(8,128)(2,1)}, f32[2048,128]{1,0:T(8,128)}, f32[128,512]{1,0:T(8,128)}) custom-call(bf16[3,2048,128]{2,1,0:T(8,128)(2,1)} %bitcast.5, bf16[3,2048,128]{2,1,0:T(8,128)(2,1)} %value.1, bf16[3,2048,128]{2,1,0:T(8,128)(2,1)} %value.1, f32[128,512]{1,0:T(8,128)} %get-tuple-element.6.weights), custom_call_target="tpu_custom_call" | custom-call | tf_op jit(solution)/shard_map/pallas_call | solution.py:603

commit v4 on v3

--- a/solution.py
+++ b/solution.py
@@ -516,11 +516,14 @@
 
     exchanged(5, 5, ALL)
 
-    def use_mix(a, z):
-        outs[2, a] = z.astype(BF)
-    collect(5, use_mix)
-    writes.append(pltpu.make_async_copy(outs.at[2], o_streams.at[2], osem.at[3]))
-    writes[-1].start()
+    gathered(5, ALL)
+    for n in range(4):
+        z = dot(cat[...], perm[:, n * 256:(n + 1) * 256]).astype(BF)
+        outs[2, 2 * n] = z[:, :128]
+        outs[2, 2 * n + 1] = z[:, 128:]
+        pair = pl.ds(2 * n, 2)
+        writes.append(pltpu.make_async_copy(outs.at[2, pair], o_streams.at[2, pair], osem.at[3 + n]))
+        writes[-1].start()
 
     for copy in sent[len(early):]:
         copy.wait_send()
@@ -583,7 +586,7 @@
             vm((4, 128, 512), BF),
             vm((3, 8, 256, 128), BF),
             vm((128, 512), F32),
-            sem((11,)), sem((5,)),
+            sem((11,)), sem((7,)),
             sem((184,)), sem((32, 12)),
             sem((8, 8)), sem((8, 8)),
             sem((13,)), sem((8,)),

time: 147 us -> 147 us (level)
  no operation moved by 1% of the time
where the time goes in v4:
time: 147 us; the launch traced here: 146 us
  Pallas kernels  146 us (99%)
    pallas_call x1, Pallas kernels, shards(): pl.pallas_call(kernel, out_shape=(jax.ShapeDtypeStruct((3, 8, 256, 128),...  143 us
    pallas_call x1, Pallas kernels, shards(): pl.pallas_call(finish, grid=(2,), out_shape=(jax.ShapeDtypeStruct((3, 204...  3.06 us

profile of v4, /device:TPU:41, one launch (start us, length us, event | category | flops | bytes accessed | tf_op | source)
XLA Modules:
  0.0 146.5 jit_solution(5146137606834971653)
XLA Ops:
  0.6 142.8 %shard_map.130 = (bf16[3,8,256,128]{3,2,1,0:T(8,128)(2,1)}, f32[128,512]{1,0:T(8,128)}) custom-call(bf16[3,8,256,128]{3,2,1,0:T(8,128)(2,1)} %bitcast.4, bf16[8,256,128]{2,1,0:T(8,128)(2,1)} %bitcast.6, bf16[8,256,128]{2,1,0:T(8,128)(2,1)} %bitcast.7, bf16[128,512]{1,0:T(8,128)(2,1)} %weight.1, bf16[1024,1024]{1,0:T(8,128)(2,1)} %constant.14.clone.perm_h, ...), custom_call_target="tpu_custom_call" | custom-call | tf_op jit(solution)/shard_map/pallas_call | solution.py:552
  143.4 3.1 %shard_map.131 = (bf16[3,2048,128]{2,1,0:T(8,128)(2,1)}, f32[2048,128]{1,0:T(8,128)}, f32[128,512]{1,0:T(8,128)}) custom-call(bf16[3,2048,128]{2,1,0:T(8,128)(2,1)} %bitcast.5, bf16[3,2048,128]{2,1,0:T(8,128)(2,1)} %value.1, bf16[3,2048,128]{2,1,0:T(8,128)(2,1)} %value.1, f32[128,512]{1,0:T(8,128)} %get-tuple-element.6.weights), custom_call_target="tpu_custom_call" | custom-call | tf_op jit(solution)/shard_map/pallas_call | solution.py:606
